TPU v7x, 128 devices: a whole 4x4x4 slice. The times are simulated.
128 devices in a mesh: seq: 4 (over x), fsdp: 16 (over z, y), dp: 2 (over core).
Axes of the slice: x: 4, y: 4, z: 4, core: 2. Of those that a mesh axis runs over, the one named last changes fastest.
Arguments:
- layer_input: bfloat16 [32, 1024, 8192], P(('fsdp', 'dp'), 'seq'), may hold values from -6 to 6
- c_weight: bfloat16 [8192, 512], P('fsdp'), may hold values from -0.0625 to 0.0625
- head_input: bfloat16 [32, 1024, 8192], P(('fsdp', 'dp'), 'seq'), may hold values from -6 to 6
- b_input: bfloat16 [32, 1024, 512], P(('fsdp', 'dp'), 'seq'), may hold values from -0.1796875 to 0.1796875
- log_decay: float32 [32, 64, 1024], P(('fsdp', 'dp'), None, 'seq'), may hold values from -1 to 0
- skip_gain: float32 [64], replicated, may hold values from 0.5 to 2
- out_grad: bfloat16 [32, 1024, 8192], P(('fsdp', 'dp'), 'seq'), may hold values from -0.29882812 to 0.29882812
Outputs:
- head_input_grad: bfloat16 [32, 1024, 8192], P(('fsdp', 'dp'), 'seq')
- b_input_grad: bfloat16 [32, 1024, 512], P(('fsdp', 'dp'), 'seq')
- c_weight_grad: float32 [8192, 512], P('fsdp')
- log_decay_grad: float32 [32, 64, 1024], P(('fsdp', 'dp'), None, 'seq')
- skip_gain_grad: float32 [64], replicated
All inputs are finite; a program needn't handle non-finite values.
Results may differ from a plain program's by a relative error of at most 0.027.
Values may be sent and summed in bfloat16 or wider, within the bound.
A program may use at most 192 MiB of HBM per device.

v0:
```python
import jax
import jax.numpy as jnp
from jax import lax
from jax.sharding import PartitionSpec as P

HEAD_COUNT = 64
P_SIZE = 128
N = 128
G = 4
BLK = 256
HG = 16
HIGHEST = lax.Precision.HIGHEST


def entering_2(array, axis, combine, identity, reverse):
    peers, index = (lax.axis_size(axis), lax.axis_index(axis))
    everything = jax.tree.map(
        lambda part, kind: lax.all_gather(part.astype(kind), axis),
        array,
        (jnp.bfloat16, jnp.bfloat16),
    )
    start = jax.tree.map(
        lambda part, zero: jnp.broadcast_to(jnp.asarray(zero, part.dtype), part.shape),
        array,
        identity,
    )

    def turn(k, before):
        at = peers - 1 - k if reverse else k
        reached = at > index if reverse else at < index
        new = combine(
            before, jax.tree.map(lambda part, own: part[at].astype(own.dtype), everything, array)
        )
        return jax.tree.map(lambda a, b: jnp.where(reached, a, b), new, before)

    return lax.fori_loop(0, peers, turn, start)


def block_forward(values, b_block, c_block, log_block, skip_gain, entering):
    length = values.shape[0]
    running = jnp.cumsum(log_block, axis=1)
    ending = running[:, -1]
    spread = running[:, :, None] - running[:, None, :]
    causal = jnp.arange(length)[:, None] >= jnp.arange(length)[None, :]
    decays = jnp.exp(jnp.where(causal[None], spread, -1e30))
    b_groups = b_block.reshape(length, G, N)
    c_groups = c_block.reshape(length, G, N)
    scores = jnp.einsum("tgn,sgn->gts", c_groups, b_groups, preferred_element_type=jnp.float32)
    mixing = (decays.reshape(G, HG, length, length) * scores[:, None]).astype(jnp.bfloat16)
    grouped = values.reshape(length, G, HG, P_SIZE)
    within = jnp.einsum("gkts,sgkp->tgkp", mixing, grouped, preferred_element_type=jnp.float32)
    from_start = jnp.exp(running).T.reshape(length, G, HG, 1)
    c_decayed = c_groups[:, :, None, :].astype(jnp.float32) * from_start
    carried = jnp.einsum(
        "tgkn,gkpn->tgkp", c_decayed, entering.reshape(G, HG, P_SIZE, N), precision=HIGHEST
    )
    to_end = jnp.exp(ending[None, :] - running.T).reshape(length, G, HG, 1)
    b_decayed = (b_groups[:, :, None, :].astype(jnp.float32) * to_end).astype(jnp.bfloat16)
    own_state = jnp.einsum(
        "sgkp,sgkn->gkpn", grouped, b_decayed, preferred_element_type=jnp.float32
    )
    leaving = jnp.exp(ending)[:, None, None] * entering + own_state.reshape(HEAD_COUNT, P_SIZE, N)
    output = (
        within + carried + skip_gain.reshape(G, HG)[None, :, :, None] * grouped.astype(jnp.float32)
    )
    return (output.reshape(length, HEAD_COUNT * P_SIZE).astype(jnp.bfloat16), leaving)


def span_forward(values, b_span, c_span, log_span, skip_gain, entering):
    blocks_here = values.shape[0] // BLK
    pieces = (
        values.reshape(blocks_here, BLK, HEAD_COUNT * P_SIZE),
        b_span.reshape(blocks_here, BLK, G * N),
        c_span.reshape(blocks_here, BLK, G * N),
        jnp.moveaxis(log_span.reshape(HEAD_COUNT, blocks_here, BLK), 1, 0),
    )

    def advance(states, block_in):
        out_block, leaving = block_forward(
            block_in[0], block_in[1], block_in[2], block_in[3], skip_gain, states
        )
        return (leaving, out_block)

    leaving, outputs = lax.scan(advance, entering, pieces)
    return (outputs.reshape(values.shape[0], HEAD_COUNT * P_SIZE), leaving)


def span_summary(values, b_span, log_span):
    length = values.shape[0]
    running = jnp.cumsum(log_span, axis=1)
    ending = running[:, -1]
    to_end = jnp.exp(ending[None, :] - running.T).reshape(length, G, HG, 1)
    b_decayed = (b_span.reshape(length, G, 1, N).astype(jnp.float32) * to_end).astype(jnp.bfloat16)
    own_state = jnp.einsum(
        "sgkp,sgkn->gkpn",
        values.reshape(length, G, HG, P_SIZE),
        b_decayed,
        preferred_element_type=jnp.float32,
    )
    return (jnp.exp(ending), own_state.reshape(HEAD_COUNT, P_SIZE, N))


def span_adjoint(grad_span, c_span, log_span):
    length = grad_span.shape[0]
    running = jnp.cumsum(log_span, axis=1)
    from_start = jnp.exp(running).T.reshape(length, G, HG, 1)
    c_decayed = (c_span.reshape(length, G, 1, N).astype(jnp.float32) * from_start).astype(
        jnp.bfloat16
    )
    adjoint = jnp.einsum(
        "tgkp,tgkn->gkpn",
        grad_span.reshape(length, G, HG, P_SIZE),
        c_decayed,
        preferred_element_type=jnp.float32,
    )
    return adjoint.reshape(HEAD_COUNT, P_SIZE, N)


def chain_link(earlier, later):
    product = earlier[0] * later[0]
    combined = later[0][:, None, None] * earlier[1] + later[1]
    return (product, combined)


def on_device(layer_input, c_weight, head_input, b_input, log_decay, skip_gain, out_grad):
    tok_rows = layer_input[0]
    columns = tok_rows
    c_span = jnp.dot(
        columns,
        lax.all_gather(c_weight, "fsdp", axis=0, tiled=True),
        preferred_element_type=jnp.float32,
    ).astype(jnp.bfloat16)
    values = head_input[0]
    b_span = b_input[0]
    log_span = log_decay[0]
    grad_span = out_grad[0]
    span_decay, own_state = span_summary(values, b_span, log_span)
    decay_wire = span_decay.astype(jnp.bfloat16).astype(jnp.float32)
    own_wire = own_state.astype(jnp.bfloat16).astype(jnp.float32)
    adjoint_wire = (
        span_adjoint(grad_span, c_span, log_span).astype(jnp.bfloat16).astype(jnp.float32)
    )
    identity = (
        jnp.ones((HEAD_COUNT,), jnp.float32),
        jnp.zeros((HEAD_COUNT, P_SIZE, N), jnp.float32),
    )
    entering = entering_2((decay_wire, own_wire), "seq", chain_link, identity, False)[1]
    leaving_grad = entering_2((decay_wire, adjoint_wire), "seq", chain_link, identity, True)[1]
    entering = lax.optimization_barrier(entering.astype(jnp.bfloat16)).astype(jnp.float32)
    leaving_grad = lax.optimization_barrier(leaving_grad.astype(jnp.bfloat16)).astype(jnp.float32)
    primal, pullback = jax.vjp(span_forward, values, b_span, c_span, log_span, skip_gain, entering)
    values_grad, b_grad, c_grad, log_grad, skip_part, enter_grad = pullback(
        (grad_span, leaving_grad)
    )
    columns = tok_rows
    grad_shard = lax.psum_scatter(
        lax.dot_general(
            columns, c_grad, (((0,), (0,)), ((), ())), preferred_element_type=jnp.float32
        ).astype(jnp.bfloat16),
        "fsdp",
        scatter_dimension=0,
        tiled=True,
    )
    weight_grad = lax.psum(grad_shard, ("seq", "dp")).astype(jnp.float32)
    documents = lax.axis_size("fsdp") * lax.axis_size("dp")
    skip_total = lax.psum(skip_part, ("seq", "fsdp", "dp"))
    return (
        values_grad[None],
        b_grad[None],
        weight_grad / documents,
        log_grad[None],
        skip_total / documents,
    )


def solution(mesh):
    in_specs = (
        P(("fsdp", "dp"), "seq", None),
        P("fsdp", None),
        P(("fsdp", "dp"), "seq", None),
        P(("fsdp", "dp"), "seq", None),
        P(("fsdp", "dp"), None, "seq"),
        P(),
        P(("fsdp", "dp"), "seq", None),
    )
    out_specs = (
        P(("fsdp", "dp"), "seq", None),
        P(("fsdp", "dp"), "seq", None),
        P("fsdp", None),
        P(("fsdp", "dp"), None, "seq"),
        P(),
    )
    return jax.shard_map(
        on_device, mesh=mesh, in_specs=in_specs, out_specs=out_specs, check_vma=False
    )
```

profile of v0, /device:TPU:0, one launch (start us, length us, event | category | flops | bytes accessed | tf_op | source)
XLA Modules:
  0.0 422.4 jit_solution(13188554458518510789)
XLA Ops:
  7.2 0.7 all-gather.5.cloned.1.call-update
  7.9 1.1 copy.185
  9.0 0.9 reshape.365
  11.2 3.6 copy.186
  14.8 4.8 %fusion.40 = bf16[4,16,128,128]{3,2,1,0:T(8,128)(2,1)S(1)} fusion(bf16[256,4,16,128]{3,2,1,0:T(8,128)(2,1)S(1)} %bitcast.145, f32[256,4,16]{0,2,1:T(8,128)S(1)} %bitcast.158, f32[256,4,128]{0,2,1:T(8,128)S(1)} %convert_element_type.256), kind=kOutput, calls=%fused_computation.57 | convolution fusion | flops 542113792 | bytes 6881280 | tf_op jit(solution)/shard_map/sgkp,sgkn->gkpn/dot_general | solution.py:94
  19.6 3.0 copy.166
  22.7 6.4 %copy.144 = bf16[1,256,8192]{1,2,0:T(8,128)(2,1)} copy(bf16[1,256,8192]{2,1,0:T(8,128)(2,1)} %param.17) | data formatting | bytes 8388608 | tf_op args[6]
  29.1 54.4 %all-gather.5.cloned.1.call-done = bf16[8192,512]{1,0:T(8,128)(2,1)} async-done(((bf16[512,512]{1,0:T(8,128)(2,1)}), bf16[8192,512]{1,0:T(8,128)(2,1)}) %all-gather.5.cloned.1.call-update) | async-done | bytes 8388624 | tf_op jit(solution)/shard_map/all_gather | solution.py:130
  83.5 7.0 %fusion.43 = bf16[256,512]{1,0:T(8,128)(2,1)S(1)} fusion(bf16[8192,512]{1,0:T(8,128)(2,1)} %all-gather.5.cloned.1.call-done, bf16[1,256,8192]{2,1,0:T(8,128)(2,1)} %param.11), kind=kOutput, calls=%fused_computation.60 | convolution fusion | flops 2147614720 | bytes 12845056 | tf_op jit(solution)/shard_map/dot_general | solution.py:128
  90.8 3.5 fusion.39
  94.2 2.9 copy.152
  97.3 0.7 reduce_window_sum.59
  99.5 10.7 %all-reduce.1 = bf16[256]{0:T(256)(128)(2,1)S(1)} all-reduce(bf16[256]{0:T(256)(128)(2,1)S(1)} %dynamic-update-slice), channel_id=2, replica_groups=mesh['seq'=4,'fsdp'=16,'dp'=2] {'seq'}, use_global_device_ids=true, to_apply=%add.1 | all-reduce | flops 256 | bytes 1024
  110.9 57.1 %all-gather.9.cloned.1.call-done = bf16[4,64,128,128]{3,2,1,0:T(8,128)(2,1)} async-done(((bf16[1,64,128,128]{3,2,1,0:T(8,128)(2,1)}), bf16[4,64,128,128]{3,2,1,0:T(8,128)(2,1)}) %all-gather.9.cloned.1.call-update) | async-done | bytes 8388624 | tf_op jit(solution)/shard_map/all_gather | solution.py:18
  168.1 23.4 %while.21 = (s32[]{:T(128)}, f32[64,128,128]{2,1,0:T(8,128)}, s32[]{:T(128)}, bf16[4,64]{1,0:T(4,128)(2,1)S(1)}, bf16[4,64,128,128]{3,2,1,0:T(8,128)(2,1)}, /*index=5*/s32[]{:T(128)}, s32[]{:T(128)}) while((s32[]{:T(128)}, f32[64,128,128]{2,1,0:T(8,128)}, s32[]{:T(128)}, bf16[4,64]{1,0:T(4,128)(2,1)S(1)}, ...), condition=%wide.region_7.8_spmd.clone, body=%wide.region_6.7_spmd.clone.sunk | while | flops 5242948 | bytes 10486513 | solution.py:36
  168.1 4.6 %fusion.74 = f32[64,128,128]{2,1,0:T(8,128)} fusion(f32[64,128,128]{2,1,0:T(8,128)} %get-tuple-element.601, bf16[4,64,128,128]{3,2,1,0:T(8,128)(2,1)} %get-tuple-element.611, s32[]{:T(128)S(6)} %copy.210, f32[64]{0:T(128)S(1)} %bitcast_convert_fusion.5, pred[]{:T(512)S(6)} %compare.8, pred[]{:T(512)S(6)} %lt.47), kind=kLoop, calls=%fused_computation.4.clone.1 | loop fusion | flops 5242880 | bytes 10486022 | tf_op jit(solution)/shard_map/while/body/eval_jaxpr/jit(_where)/select_n | solution.py:34
  172.7 5.9 %fusion.74 = f32[64,128,128]{2,1,0:T(8,128)} fusion(f32[64,128,128]{2,1,0:T(8,128)} %get-tuple-element.601, bf16[4,64,128,128]{3,2,1,0:T(8,128)(2,1)} %get-tuple-element.611, s32[]{:T(128)S(6)} %copy.210, f32[64]{0:T(128)S(1)} %bitcast_convert_fusion.5, pred[]{:T(512)S(6)} %compare.8, pred[]{:T(512)S(6)} %lt.47), kind=kLoop, calls=%fused_computation.4.clone.1 | loop fusion | flops 5242880 | bytes 10486022 | tf_op jit(solution)/shard_map/while/body/eval_jaxpr/jit(_where)/select_n | solution.py:34
  178.6 6.7 %fusion.74 = f32[64,128,128]{2,1,0:T(8,128)} fusion(f32[64,128,128]{2,1,0:T(8,128)} %get-tuple-element.601, bf16[4,64,128,128]{3,2,1,0:T(8,128)(2,1)} %get-tuple-element.611, s32[]{:T(128)S(6)} %copy.210, f32[64]{0:T(128)S(1)} %bitcast_convert_fusion.5, pred[]{:T(512)S(6)} %compare.8, pred[]{:T(512)S(6)} %lt.47), kind=kLoop, calls=%fused_computation.4.clone.1 | loop fusion | flops 5242880 | bytes 10486022 | tf_op jit(solution)/shard_map/while/body/eval_jaxpr/jit(_where)/select_n | solution.py:34
  185.4 6.1 %fusion.74 = f32[64,128,128]{2,1,0:T(8,128)} fusion(f32[64,128,128]{2,1,0:T(8,128)} %get-tuple-element.601, bf16[4,64,128,128]{3,2,1,0:T(8,128)(2,1)} %get-tuple-element.611, s32[]{:T(128)S(6)} %copy.210, f32[64]{0:T(128)S(1)} %bitcast_convert_fusion.5, pred[]{:T(512)S(6)} %compare.8, pred[]{:T(512)S(6)} %lt.47), kind=kLoop, calls=%fused_computation.4.clone.1 | loop fusion | flops 5242880 | bytes 10486022 | tf_op jit(solution)/shard_map/while/body/eval_jaxpr/jit(_where)/select_n | solution.py:34
  191.4 2.6 convert_element_type.274
  194.6 5.0 %fusion.10 = (f32[256,4,16]{0,2,1:T(8,128)}, bf16[256,4,128]{0,2,1:T(8,128)(2,1)S(1)}) fusion(f32[256,4,128]{0,2,1:T(8,128)S(1)} %copy.148, f32[256,4,16]{0,2,1:T(8,128)} %bitcast.162, bf16[4,16,128,128]{3,2,1,0:T(8,128)(2,1)S(1)} %bitcast.134, bf16[4,16,128,256]{3,2,1,0:T(8,128)(2,1)} %bitcast.141), kind=kOutput, calls=%fused_computation.21 | convolution fusion | flops 545112064 | bytes 7208960 | tf_op jit(solution)/shard_map/transpose(jvp())/while/body/eval_jaxpr/tgkn,gkpn->tgkp/dot_general | solution.py:54
  199.8 18.1 %fusion.6 = (f32[4,16,256]{2,1,0:T(8,128)}, f32[4,16,256]{2,1,0:T(8,128)}, bf16[4,256,256]{2,1,0:T(8,128)(2,1)S(1)}) fusion(f32[4,256,256]{2,1,0:T(8,128)S(1)} %fusion.55, f32[4,16,256]{2,1,0:T(8,128)S(1)} %copy-done.17, pred[256,256]{1,0:T(8,128)(4,1)S(1)} %copy-done.19, bf16[4,16,128,256]{3,2,1,0:T(8,128)(2,1)S(1)} %bitcast.144, ...), kind=kOutput, calls=%fused_computation.14 | convolution fusion | flops 1119584256 | bytes 10223616 | tf_op jit(solution)/shard_map/transpose(jvp())/while/body/eval_jaxpr/gkts,sgkp->tgkp/dot_general | solution.py:51
  218.2 5.6 %fusion.7 = bf16[8192,512]{0,1:T(8,128)(2,1)} fusion(bf16[256,512]{0,1:T(8,128)(2,1)S(1)} %bitcast.153, bf16[1,256,8192]{2,1,0:T(8,128)(2,1)S(1)} %copy-done.1), kind=kOutput, calls=%fused_computation.16 | convolution fusion | flops 2151677952 | bytes 12845056 | tf_op jit(solution)/shard_map/dot_general | solution.py:157
  224.5 4.9 %multiply_reduce_fusion = f32[8192]{0:T(1024)S(1)} fusion(bf16[1,256,8192]{2,1,0:T(8,128)(2,1)} %param.13, bf16[1,256,8192]{2,1,0:T(8,128)(2,1)} %param.17), kind=kLoop, calls=%fused_computation.26 | loop fusion | flops 8380416 | bytes 8421376 | tf_op jit(solution)/shard_map/transpose(jvp())/while/body/eval_jaxpr/reduce_sum | solution.py:64
  229.7 67.1 %psum.15 = f32[64]{0:T(128)S(1)} all-reduce(f32[64]{0:T(128)S(1)} %reshape.375), channel_id=1, replica_groups=mesh['seq'=4,'fsdp'=16,'dp'=2] {'seq','fsdp','dp'}, use_global_device_ids=true, to_apply=%region_21.22 | all-reduce | flops 64 | bytes 512 | tf_op jit(solution)/shard_map/psum | solution.py:166
  297.3 0.8 copy.172
  298.1 0.8 copy.171
  298.8 0.7 copy.170
  299.6 7.3 %fusion.8 = bf16[4,16,256,128]{2,3,1,0:T(8,128)(2,1)} fusion(bf16[4,16,128,256]{3,2,1,0:T(8,128)(2,1)} %bitcast.142, f32[4,256,256]{2,1,0:T(8,128)} %copy-done.6, f32[4,16,256]{2,1,0:T(8,128)S(1)} %copy-done.18, pred[256,256]{1,0:T(8,128)(4,1)S(1)} %copy-done.20), kind=kOutput, calls=%fused_computation.17 | convolution fusion | flops 1090519040 | bytes 9568256 | tf_op jit(solution)/shard_map/transpose(jvp())/while/body/eval_jaxpr/gkts,sgkp->tgkp/dot_general | solution.py:51
  306.9 22.8 %while.20 = (s32[]{:T(128)}, f32[64,128,128]{2,1,0:T(8,128)}, s32[]{:T(128)}, bf16[4,64]{1,0:T(4,128)(2,1)S(1)}, bf16[4,64,128,128]{3,2,1,0:T(8,128)(2,1)}, /*index=5*/s32[]{:T(128)}, s32[]{:T(128)}, s32[]{:T(128)}, s32[]{:T(128)}) while((s32[]{:T(128)}, f32[64,128,128]{2,1,0:T(8,128)}, s32[]{:T(128)}, ...), condition=%wide.region_3.4_spmd.clone, body=%wide.region_2.3_spmd.clone.sunk | while | flops 5242952 | bytes 10486575 | solution.py:36
  306.9 4.8 %fusion.73 = f32[64,128,128]{2,1,0:T(8,128)} fusion(f32[64,128,128]{2,1,0:T(8,128)} %get-tuple-element.576, bf16[4,64,128,128]{3,2,1,0:T(8,128)(2,1)} %get-tuple-element.588, s32[]{:T(128)S(6)} %select_n.103, f32[64]{0:T(128)S(1)} %bitcast_convert_fusion.4, pred[]{:T(512)S(6)} %compare.7, pred[]{:T(512)S(6)} %gt.12), kind=kLoop, calls=%fused_computation.1.clone.1 | loop fusion | flops 5242880 | bytes 10486022 | tf_op jit(solution)/shard_map/while/body/eval_jaxpr/jit(_where)/select_n | solution.py:34
  311.7 6.0 %fusion.73 = f32[64,128,128]{2,1,0:T(8,128)} fusion(f32[64,128,128]{2,1,0:T(8,128)} %get-tuple-element.576, bf16[4,64,128,128]{3,2,1,0:T(8,128)(2,1)} %get-tuple-element.588, s32[]{:T(128)S(6)} %select_n.103, f32[64]{0:T(128)S(1)} %bitcast_convert_fusion.4, pred[]{:T(512)S(6)} %compare.7, pred[]{:T(512)S(6)} %gt.12), kind=kLoop, calls=%fused_computation.1.clone.1 | loop fusion | flops 5242880 | bytes 10486022 | tf_op jit(solution)/shard_map/while/body/eval_jaxpr/jit(_where)/select_n | solution.py:34
  317.7 6.0 %fusion.73 = f32[64,128,128]{2,1,0:T(8,128)} fusion(f32[64,128,128]{2,1,0:T(8,128)} %get-tuple-element.576, bf16[4,64,128,128]{3,2,1,0:T(8,128)(2,1)} %get-tuple-element.588, s32[]{:T(128)S(6)} %select_n.103, f32[64]{0:T(128)S(1)} %bitcast_convert_fusion.4, pred[]{:T(512)S(6)} %compare.7, pred[]{:T(512)S(6)} %gt.12), kind=kLoop, calls=%fused_computation.1.clone.1 | loop fusion | flops 5242880 | bytes 10486022 | tf_op jit(solution)/shard_map/while/body/eval_jaxpr/jit(_where)/select_n | solution.py:34
  323.7 5.9 %fusion.73 = f32[64,128,128]{2,1,0:T(8,128)} fusion(f32[64,128,128]{2,1,0:T(8,128)} %get-tuple-element.576, bf16[4,64,128,128]{3,2,1,0:T(8,128)(2,1)} %get-tuple-element.588, s32[]{:T(128)S(6)} %select_n.103, f32[64]{0:T(128)S(1)} %bitcast_convert_fusion.4, pred[]{:T(512)S(6)} %compare.7, pred[]{:T(512)S(6)} %gt.12), kind=kLoop, calls=%fused_computation.1.clone.1 | loop fusion | flops 5242880 | bytes 10486022 | tf_op jit(solution)/shard_map/while/body/eval_jaxpr/jit(_where)/select_n | solution.py:34
  329.7 2.7 convert_element_type.255
  332.4 0.7 copy-done.5
  333.2 6.1 %fusion.12 = (f32[256,4,16]{0,2,1:T(8,128)}, bf16[256,4,128]{0,2,1:T(8,128)(2,1)}) fusion(f32[256,4,128]{0,2,1:T(8,128)S(1)} %copy-done.8, f32[256,4,16]{0,2,1:T(8,128)S(1)} %bitcast.160, bf16[4,16,128,128]{3,2,1,0:T(8,128)(2,1)S(1)} %bitcast.135, bf16[256,4,16,128]{3,2,1,0:T(8,128)(2,1)S(1)} %bitcast.147), kind=kOutput, calls=%fused_computation.25 | convolution fusion | flops 549306368 | bytes 7208960 | tf_op jit(solution)/shard_map/transpose(jvp())/while/body/eval_jaxpr/sgkp,sgkn->gkpn/dot_general | solution.py:59
  339.3 1.0 copy.169
  340.4 2.4 multiply_reduce_fusion.1
  343.0 2.5 reduce-window.24
  345.5 1.2 fusion.49
  346.7 8.7 %fusion.21 = bf16[256,4,16,128]{0,3,2,1:T(8,128)(2,1)} fusion(bf16[256,4,16,128]{0,3,2,1:T(8,128)(2,1)} %bitcast.143, bf16[4,16,256,128]{2,3,1,0:T(8,128)(2,1)} %fusion.8, f32[4,16]{1,0:T(4,128)S(1)} %mul.237, bf16[4,16,128,128]{3,2,1,0:T(8,128)(2,1)} %bitcast.136, f32[256,4,16]{0,2,1:T(8,128)} %bitcast.159, f32[256,4,128]{0,2,1:T(8,128)} %copy-done.7), kind=kOutput, calls=%fused_computation.39 | convolution fusion | flops 553648128 | bytes 15270144 | tf_op jit(solution)/shard_map/transpose(jvp())/while/body/eval_jaxpr/sgkp,sgkn->gkpn/dot_general | solution.py:59
  355.5 6.3 %copy.175 = bf16[1,256,8192]{2,1,0:T(8,128)(2,1)} copy(bf16[1,256,8192]{1,2,0:T(8,128)(2,1)} %bitcast.148) | data formatting | bytes 8388608
  361.8 0.8 copy.176
  362.9 0.7 reduce_window_sum.61
  363.6 49.8 %all-reduce.4.cloned.1.call-done = bf16[512,512]{0,1:T(8,128)(2,1)} async-done(((bf16[512,512]{0,1:T(8,128)(2,1)}), bf16[512,512]{0,1:T(8,128)(2,1)}) %all-reduce.4.cloned.1.call-update) | async-done | bytes 524304 | tf_op jit(solution)/shard_map/psum | solution.py:164
  413.4 1.2 convert_multiply_fusion.2
  414.6 1.3 copy.177
  (105 shorter events, 6.4 us)
Async XLA Ops:
  7.2 76.3 %all-gather.5.cloned.1.call-start = ((), (), s32[]{:S(2)}) async-start(), calls=%async_computation.1 | async-start | bytes 8912896 | tf_op jit(solution)/shard_map/all_gather | solution.py:130
  7.9 160.2 %all-gather.9.cloned.1.call-start = ((), (), s32[]{:S(2)}) async-start(), calls=%async_computation.3 | async-start | bytes 10485760 | tf_op jit(solution)/shard_map/all_gather | solution.py:18
  11.1 3.7 copy-start.12
  11.2 3.6 copy-start.7
  14.7 4.9 %copy-start.3 = (bf16[32,8,64,128]{3,2,1,0:T(8,128)(2,1)}, bf16[32,8,64,128]{3,2,1,0:T(8,128)(2,1)S(1)}, u32[]{:S(2)}) copy-start(bf16[32,8,64,128]{3,2,1,0:T(8,128)(2,1)S(1)} %copy.186) | copy-start | bytes 12582916
  22.6 284.3 %all-gather.7.cloned.1.call-start = ((), (), s32[]{:S(2)}) async-start(), calls=%async_computation.2 | async-start | bytes 10485760 | tf_op jit(solution)/shard_map/all_gather | solution.py:18
  29.1 61.6 %copy-start.14 = (f32[256,64]{0,1:T(8,128)}, f32[256,64]{0,1:T(8,128)S(1)}, u32[]{:S(2)}) copy-start(f32[256,64]{0,1:T(8,128)S(1)} %copy.150) | copy-start | bytes 196612
  94.2 3.8 copy-start.23
  97.2 258.2 %reduce-scatter.2.cloned.1.call-start = ((), (), s32[]{:S(2)}) async-start(), calls=%async_computation.4 | async-start | bytes 8912896 | tf_op jit(solution)/shard_map/reduce_scatter | solution.py:156
  194.6 5.1 %copy-start.6 = (f32[4,256,256]{2,1,0:T(8,128)}, f32[4,256,256]{2,1,0:T(8,128)S(1)}, u32[]{:S(2)}) copy-start(f32[4,256,256]{2,1,0:T(8,128)S(1)} %fusion.55) | copy-start | bytes 3145732
  194.6 5.1 %copy-start.2 = (bf16[1,256,8192]{1,2,0:T(8,128)(2,1)S(1)}, bf16[1,256,8192]{1,2,0:T(8,128)(2,1)}, u32[]{:S(2)}) copy-start(bf16[1,256,8192]{1,2,0:T(8,128)(2,1)} %copy.144) | copy-start | bytes 12582916
  194.6 5.2 %copy-start.4 = (bf16[32,8,64,128]{3,2,1,0:T(8,128)(2,1)S(1)}, bf16[32,8,64,128]{3,2,1,0:T(8,128)(2,1)}, u32[]{:S(2)}) copy-start(bf16[32,8,64,128]{3,2,1,0:T(8,128)(2,1)} %copy-done.3) | copy-start | bytes 12582916
  194.6 5.2 %copy-start.17 = (f32[4,16,256]{2,1,0:T(8,128)S(1)}, f32[4,16,256]{2,1,0:T(8,128)}, u32[]{:S(2)}) copy-start(f32[4,16,256]{2,1,0:T(8,128)} %reduce_window_sum.59) | copy-start | bytes 196612
  194.6 5.1 %copy-start.19 = (pred[256,256]{1,0:T(8,128)(4,1)S(1)}, pred[256,256]{1,0:T(8,128)(4,1)}, u32[]{:S(2)}) copy-start(pred[256,256]{1,0:T(8,128)(4,1)} %iota_compare_fusion) | copy-start | bytes 196612
  199.8 18.4 %copy-start.1 = (bf16[1,256,8192]{2,1,0:T(8,128)(2,1)S(1)}, bf16[1,256,8192]{2,1,0:T(8,128)(2,1)}, u32[]{:S(2)}) copy-start(bf16[1,256,8192]{2,1,0:T(8,128)(2,1)} %param.11) | copy-start | bytes 12582916
  223.8 0.7 copy-start.22
  223.8 189.6 %all-reduce.4.cloned.1.call-start = ((), (), s32[]{:S(2)}) async-start(), calls=%async_computation.5 | async-start | bytes 1048576 | tf_op jit(solution)/shard_map/psum | solution.py:164
  224.5 72.8 %copy-start.16 = (f32[4,16,256]{2,1,0:T(8,128)S(1)}, f32[4,16,256]{2,1,0:T(8,128)}, u32[]{:S(2)}) copy-start(f32[4,16,256]{2,1,0:T(8,128)} %get-tuple-element.474) | copy-start | bytes 196612
  224.5 73.5 %copy-start.21 = (f32[4,16,256]{2,1,0:T(8,128)S(1)}, f32[4,16,256]{2,1,0:T(8,128)}, u32[]{:S(2)}) copy-start(f32[4,16,256]{2,1,0:T(8,128)} %get-tuple-element.473) | copy-start | bytes 196612
  224.5 74.3 %copy-start.15 = (f32[256,4,16]{0,2,1:T(8,128)S(1)}, f32[256,4,16]{0,2,1:T(8,128)}, u32[]{:S(2)}) copy-start(f32[256,4,16]{0,2,1:T(8,128)} %get-tuple-element.476) | copy-start | bytes 196612
  224.5 75.1 %copy-start.18 = (f32[4,16,256]{2,1,0:T(8,128)S(1)}, f32[4,16,256]{2,1,0:T(8,128)}, u32[]{:S(2)}) copy-start(f32[4,16,256]{2,1,0:T(8,128)} %reduce_window_sum.59) | copy-start | bytes 196612
  224.5 75.1 %copy-start.20 = (pred[256,256]{1,0:T(8,128)(4,1)S(1)}, pred[256,256]{1,0:T(8,128)(4,1)}, u32[]{:S(2)}) copy-start(pred[256,256]{1,0:T(8,128)(4,1)} %iota_compare_fusion) | copy-start | bytes 196612
  329.7 3.4 copy-start.5
  329.7 3.6 copy-start.8
  329.7 3.6 copy-start.13
  332.4 6.9 %copy-start = (bf16[64,128,128]{2,1,0:T(8,128)(2,1)}, bf16[64,128,128]{2,1,0:T(8,128)(2,1)S(1)}, u32[]{:S(2)}) copy-start(bf16[64,128,128]{2,1,0:T(8,128)(2,1)S(1)} %convert_element_type.255) | copy-start | bytes 6291460
  339.3 3.5 copy-start.9
  339.3 3.5 copy-start.10
  339.3 3.5 copy-start.11
Sparse Core Ops, SparseCore 0:
  10.1 73.3 all-gather.4
  85.2 82.8 all-gather.8
  169.7 84.7 all-gather.6
  257.8 86.5 reduce-scatter.1
  355.5 57.8 all-reduce.3
where the time goes:
time: 423 us; the launch traced here: 422 us
  waiting for transfers between devices  162 us (38%)
  blocking collectives  77.8 us (18%)
  matrix products  67.9 us (16%)
  other arithmetic  64.8 us (15%)
  local copies, waits for them, and re-layouts  34.7 us (8%)
  between operations  14.9 us (4%)
    psum x1, blocking collectives, on_device(): skip_total = lax.psum(skip_part, ('seq', 'fsdp', 'dp'))  67.1 us
    all_gather x2, waiting for transfers between devices, entering_2(): lax.all_gather(part.astype(kind), axis)  57.1 us
    all_gather x1, waiting for transfers between devices, on_device(): lax.all_gather(c_weight, 'fsdp', axis=0, tiled=True)  54.4 us
    psum x1, waiting for transfers between devices, on_device(): weight_grad = lax.psum(grad_shard, ('seq', 'dp')).astype(jnp.float32)  49.8 us
    select_n x8, other arithmetic, turn(): return jax.tree.map(lambda a, b: jnp.where(reached, a, b), new, before)  46.1 us
    dot_general x2, matrix products, block_forward(): jnp.einsum('gkts,sgkp->tgkp', mixing, grouped, preferred_element_type=jnp...  25.4 us
    unnamed x56, local copies, waits for them, and re-layouts  20.9 us
    dot_general x2, matrix products, block_forward(): jnp.einsum('sgkp,sgkn->gkpn', grouped, b_decayed, preferred_element_type=...  14.8 us
  transfers between devices with their start and end apart: 5, of which 3 were waited for; matrix products, arithmetic and copies ran while one was open for 39% of the time, Pallas kernels for 0%

commit v1 on v0

--- a/solution.py
+++ b/solution.py
@@ -127,7 +127,9 @@
     columns = tok_rows
     c_span = jnp.dot(
         columns,
-        lax.all_gather(c_weight, "fsdp", axis=0, tiled=True),
+        jnp.concatenate(
+            lax.all_to_all(jnp.stack([c_weight] * lax.axis_size("fsdp")), "fsdp", 0, 0), axis=0
+        ),
         preferred_element_type=jnp.float32,
     ).astype(jnp.bfloat16)
     values = head_input[0]

time: 423 us -> 452 us (1.069); the launches traced: 422 us -> 443 us
  starting transfers between devices: 0.2 us -> 8.35 us
  waiting for transfers between devices: 162 us -> 168 us
  blocking collectives: 77.8 us -> 83.6 us
    all_to_all x0 -> x1, waiting for transfers between devices: none -> 117 us  [on_device(): lax.all_to_all(jnp.stack([c_weight] * lax.axis_size('fsdp')), 'fsdp', 0, 0)]
    all_gather x2, waiting for transfers between devices: 57.1 us -> 0.02 us  [entering_2(): lax.all_gather(part.astype(kind), axis)]
    all_gather x1 -> x0, waiting for transfers between devices: 54.4 us -> none  [on_device(): lax.all_gather(c_weight, 'fsdp', axis=0, tiled=True)]
    unnamed x1, blocking collectives: 10.7 us -> 20.8 us
    all_to_all x0 -> x1, starting transfers between devices: none -> 8.18 us  [on_device(): lax.all_to_all(jnp.stack([c_weight] * lax.axis_size('fsdp')), 'fsdp', 0, 0)]
    unnamed x56 -> x42, local copies, waits for them, and re-layouts: 20.9 us -> 22.7 us
  transfers between devices with their start and end apart: 5 -> 5, of which waited for: 3 -> 2; matrix products, arithmetic and copies ran while one was open for 39% -> 33% of each run, Pallas kernels for 0% -> 0%
where the time goes in v1:
time: 452 us; the launch traced here: 443 us
  waiting for transfers between devices  168 us (37%)
  blocking collectives  83.6 us (18%)
  matrix products  65.4 us (14%)
  other arithmetic  63.7 us (14%)
  local copies, waits for them, and re-layouts  39.1 us (9%)
  between operations  15.2 us (3%)
  starting transfers between devices  8.35 us (2%)
    all_to_all x1, waiting for transfers between devices, on_device(): lax.all_to_all(jnp.stack([c_weight] * lax.axis_size('fsdp')), 'fsdp', 0, 0)  117 us
    psum x1, blocking collectives, on_device(): skip_total = lax.psum(skip_part, ('seq', 'fsdp', 'dp'))  62.8 us
    psum x1, waiting for transfers between devices, on_device(): weight_grad = lax.psum(grad_shard, ('seq', 'dp')).astype(jnp.float32)  50.2 us
    select_n x8, other arithmetic, turn(): return jax.tree.map(lambda a, b: jnp.where(reached, a, b), new, before)  45.5 us
    dot_general x2, matrix products, block_forward(): jnp.einsum('gkts,sgkp->tgkp', mixing, grouped, preferred_element_type=jnp...  23.8 us
    unnamed x42, local copies, waits for them, and re-layouts  22.7 us
    unnamed x1, blocking collectives  20.8 us
    dot_general x2, matrix products, block_forward(): jnp.einsum('sgkp,sgkn->gkpn', grouped, b_decayed, preferred_element_type=...  14.7 us
  transfers between devices with their start and end apart: 5, of which 2 were waited for; matrix products, arithmetic and copies ran while one was open for 33% of the time, Pallas kernels for 0%

profile of v1, /device:TPU:0, one launch (start us, length us, event | category | flops | bytes accessed | tf_op | source)
XLA Modules:
  0.0 442.9 jit_solution(14334928876590309955)
XLA Ops:
  7.2 1.1 copy.185
  8.3 0.9 reshape.370
  9.2 0.6 reduce-window.16
  10.4 3.6 copy.186
  14.0 4.8 %fusion.40 = bf16[4,16,128,128]{3,2,1,0:T(8,128)(2,1)S(1)} fusion(bf16[256,4,16,128]{3,2,1,0:T(8,128)(2,1)S(1)} %bitcast.146, f32[256,4,16]{0,2,1:T(8,128)S(1)} %bitcast.159, f32[256,4,128]{0,2,1:T(8,128)S(1)} %convert_element_type.256), kind=kOutput, calls=%fused_computation.57 | convolution fusion | flops 542113792 | bytes 6881280 | tf_op jit(solution)/shard_map/sgkp,sgkn->gkpn/dot_general | solution.py:94
  18.9 2.9 copy.166
  21.9 4.0 stack.2
  25.9 8.2 %all-to-all-start = ((bf16[16,512,512]{2,1,0:T(8,128)(2,1)}), bf16[16,512,512]{2,1,0:T(8,128)(2,1)}, u32[]{:S(2)}, u32[]{:S(2)}) async-start(bf16[16,512,512]{2,1,0:T(8,128)(2,1)} %stack.2), calls=%async_computation | async-start | bytes 16777216 | tf_op jit(solution)/shard_map/all_to_all | solution.py:131
  34.1 6.6 %copy.144 = bf16[1,256,8192]{1,2,0:T(8,128)(2,1)} copy(bf16[1,256,8192]{2,1,0:T(8,128)(2,1)} %param.17) | data formatting | bytes 8388608 | tf_op args[6]
  40.8 117.3 %all-to-all-done = bf16[16,512,512]{2,1,0:T(8,128)(2,1)} async-done(((bf16[16,512,512]{2,1,0:T(8,128)(2,1)}), bf16[16,512,512]{2,1,0:T(8,128)(2,1)}, u32[]{:S(2)}, u32[]{:S(2)}) %all-to-all-start) | async-done | bytes 8388640 | tf_op jit(solution)/shard_map/all_to_all | solution.py:131
  158.1 7.0 %fusion.43 = bf16[256,512]{1,0:T(8,128)(2,1)S(1)} fusion(bf16[8192,512]{1,0:T(8,128)(2,1)} %bitcast.4, bf16[1,256,8192]{2,1,0:T(8,128)(2,1)} %param.11), kind=kOutput, calls=%fused_computation.60 | convolution fusion | flops 2147614720 | bytes 12845056 | tf_op jit(solution)/shard_map/dot_general | solution.py:128
  165.4 5.0 %fusion.39 = bf16[4,16,128,128]{3,2,1,0:T(8,128)(2,1)} fusion(bf16[256,4,16,128]{0,3,2,1:T(8,128)(2,1)} %bitcast.141, f32[256,4,16]{0,2,1:T(8,128)S(1)} %bitcast.162, f32[256,4,128]{0,2,1:T(8,128)S(1)} %copy.148), kind=kOutput, calls=%fused_computation.56 | convolution fusion | flops 542113792 | bytes 6881280 | tf_op jit(solution)/shard_map/tgkp,tgkn->gkpn/dot_general | solution.py:110
  170.4 4.1 copy.152
  174.7 0.6 dynamic-slice.11
  176.2 20.8 %all-reduce.1 = bf16[256]{0:T(256)(128)(2,1)S(1)} all-reduce(bf16[256]{0:T(256)(128)(2,1)S(1)} %dynamic-update-slice), channel_id=2, replica_groups=mesh['seq'=4,'fsdp'=16,'dp'=2] {'seq'}, use_global_device_ids=true, to_apply=%add.1 | all-reduce | flops 256 | bytes 1024
  197.6 1.0 copy-done.5
  198.6 16.5 %fusion.6 = (f32[4,16,256]{2,1,0:T(8,128)}, f32[4,16,256]{2,1,0:T(8,128)S(1)}, bf16[4,256,256]{2,1,0:T(8,128)(2,1)S(1)}) fusion(f32[4,256,256]{2,1,0:T(8,128)S(1)} %fusion.55, f32[4,16,256]{2,1,0:T(8,128)S(1)} %reduce_window_sum.59, pred[256,256]{1,0:T(8,128)(4,1)S(1)} %iota_compare_fusion, bf16[4,16,128,256]{3,2,1,0:T(8,128)(2,1)} %bitcast.142, ...), kind=kOutput, calls=%fused_computation.14 | convolution fusion | flops 1119584256 | bytes 10223616 | tf_op jit(solution)/shard_map/transpose(jvp())/while/body/eval_jaxpr/gkts,sgkp->tgkp/dot_general | solution.py:51
  215.1 22.5 %while.21 = (s32[]{:T(128)}, f32[64,128,128]{2,1,0:T(8,128)}, s32[]{:T(128)}, bf16[4,64]{1,0:T(4,128)(2,1)S(1)}, bf16[4,64,128,128]{3,2,1,0:T(8,128)(2,1)}, /*index=5*/s32[]{:T(128)}, s32[]{:T(128)}) while((s32[]{:T(128)}, f32[64,128,128]{2,1,0:T(8,128)}, s32[]{:T(128)}, bf16[4,64]{1,0:T(4,128)(2,1)S(1)}, ...), condition=%wide.region_7.8_spmd.clone, body=%wide.region_6.7_spmd.clone.sunk | while | flops 5242948 | bytes 10486513 | solution.py:36
  215.1 4.6 %fusion.74 = f32[64,128,128]{2,1,0:T(8,128)} fusion(f32[64,128,128]{2,1,0:T(8,128)} %get-tuple-element.601, bf16[4,64,128,128]{3,2,1,0:T(8,128)(2,1)} %get-tuple-element.611, s32[]{:T(128)S(6)} %copy.210, f32[64]{0:T(128)S(1)} %bitcast_convert_fusion.5, pred[]{:T(512)S(6)} %compare.8, pred[]{:T(512)S(6)} %lt.47), kind=kLoop, calls=%fused_computation.4.clone.1 | loop fusion | flops 5242880 | bytes 10486022 | tf_op jit(solution)/shard_map/while/body/eval_jaxpr/jit(_where)/select_n | solution.py:34
  219.7 6.0 %fusion.74 = f32[64,128,128]{2,1,0:T(8,128)} fusion(f32[64,128,128]{2,1,0:T(8,128)} %get-tuple-element.601, bf16[4,64,128,128]{3,2,1,0:T(8,128)(2,1)} %get-tuple-element.611, s32[]{:T(128)S(6)} %copy.210, f32[64]{0:T(128)S(1)} %bitcast_convert_fusion.5, pred[]{:T(512)S(6)} %compare.8, pred[]{:T(512)S(6)} %lt.47), kind=kLoop, calls=%fused_computation.4.clone.1 | loop fusion | flops 5242880 | bytes 10486022 | tf_op jit(solution)/shard_map/while/body/eval_jaxpr/jit(_where)/select_n | solution.py:34
  225.7 5.9 %fusion.74 = f32[64,128,128]{2,1,0:T(8,128)} fusion(f32[64,128,128]{2,1,0:T(8,128)} %get-tuple-element.601, bf16[4,64,128,128]{3,2,1,0:T(8,128)(2,1)} %get-tuple-element.611, s32[]{:T(128)S(6)} %copy.210, f32[64]{0:T(128)S(1)} %bitcast_convert_fusion.5, pred[]{:T(512)S(6)} %compare.8, pred[]{:T(512)S(6)} %lt.47), kind=kLoop, calls=%fused_computation.4.clone.1 | loop fusion | flops 5242880 | bytes 10486022 | tf_op jit(solution)/shard_map/while/body/eval_jaxpr/jit(_where)/select_n | solution.py:34
  231.6 5.9 %fusion.74 = f32[64,128,128]{2,1,0:T(8,128)} fusion(f32[64,128,128]{2,1,0:T(8,128)} %get-tuple-element.601, bf16[4,64,128,128]{3,2,1,0:T(8,128)(2,1)} %get-tuple-element.611, s32[]{:T(128)S(6)} %copy.210, f32[64]{0:T(128)S(1)} %bitcast_convert_fusion.5, pred[]{:T(512)S(6)} %compare.8, pred[]{:T(512)S(6)} %lt.47), kind=kLoop, calls=%fused_computation.4.clone.1 | loop fusion | flops 5242880 | bytes 10486022 | tf_op jit(solution)/shard_map/while/body/eval_jaxpr/jit(_where)/select_n | solution.py:34
  237.6 2.8 convert_element_type.274
  240.3 0.7 copy-done.2
  241.2 2.7 fusion.10
  244.3 5.6 %fusion.7 = bf16[8192,512]{0,1:T(8,128)(2,1)} fusion(bf16[256,512]{0,1:T(8,128)(2,1)S(1)} %bitcast.154, bf16[1,256,8192]{2,1,0:T(8,128)(2,1)S(1)} %copy-done.1), kind=kOutput, calls=%fused_computation.16 | convolution fusion | flops 2151677952 | bytes 12845056 | tf_op jit(solution)/shard_map/dot_general | solution.py:159
  250.6 4.9 %multiply_reduce_fusion = f32[8192]{0:T(1024)S(1)} fusion(bf16[1,256,8192]{2,1,0:T(8,128)(2,1)} %param.13, bf16[1,256,8192]{2,1,0:T(8,128)(2,1)} %param.17), kind=kLoop, calls=%fused_computation.26 | loop fusion | flops 8380416 | bytes 8421376 | tf_op jit(solution)/shard_map/transpose(jvp())/while/body/eval_jaxpr/reduce_sum | solution.py:64
  255.6 62.8 %psum.15 = f32[64]{0:T(128)S(1)} all-reduce(f32[64]{0:T(128)S(1)} %reshape.381), channel_id=1, replica_groups=mesh['seq'=4,'fsdp'=16,'dp'=2] {'seq','fsdp','dp'}, use_global_device_ids=true, to_apply=%region_21.22 | all-reduce | flops 64 | bytes 512 | tf_op jit(solution)/shard_map/psum | solution.py:168
  319.1 7.3 %fusion.8 = bf16[4,16,256,128]{2,3,1,0:T(8,128)(2,1)} fusion(bf16[4,16,128,256]{3,2,1,0:T(8,128)(2,1)} %bitcast.143, f32[4,256,256]{2,1,0:T(8,128)} %copy-done.5, f32[4,16,256]{2,1,0:T(8,128)S(1)} %reduce_window_sum.59, pred[256,256]{1,0:T(8,128)(4,1)S(1)} %iota_compare_fusion), kind=kOutput, calls=%fused_computation.17 | convolution fusion | flops 1090519040 | bytes 9568256 | tf_op jit(solution)/shard_map/transpose(jvp())/while/body/eval_jaxpr/gkts,sgkp->tgkp/dot_general | solution.py:51
  326.5 23.1 %while.20 = (s32[]{:T(128)}, f32[64,128,128]{2,1,0:T(8,128)}, s32[]{:T(128)}, bf16[4,64]{1,0:T(4,128)(2,1)S(1)}, bf16[4,64,128,128]{3,2,1,0:T(8,128)(2,1)}, /*index=5*/s32[]{:T(128)}, s32[]{:T(128)}, s32[]{:T(128)}, s32[]{:T(128)}) while((s32[]{:T(128)}, f32[64,128,128]{2,1,0:T(8,128)}, s32[]{:T(128)}, ...), condition=%wide.region_3.4_spmd.clone, body=%wide.region_2.3_spmd.clone.sunk | while | flops 5242952 | bytes 10486575 | solution.py:36
  326.5 4.6 %fusion.73 = f32[64,128,128]{2,1,0:T(8,128)} fusion(f32[64,128,128]{2,1,0:T(8,128)} %get-tuple-element.576, bf16[4,64,128,128]{3,2,1,0:T(8,128)(2,1)} %get-tuple-element.588, s32[]{:T(128)S(6)} %select_n.103, f32[64]{0:T(128)S(1)} %bitcast_convert_fusion.4, pred[]{:T(512)S(6)} %compare.7, pred[]{:T(512)S(6)} %gt.12), kind=kLoop, calls=%fused_computation.1.clone.1 | loop fusion | flops 5242880 | bytes 10486022 | tf_op jit(solution)/shard_map/while/body/eval_jaxpr/jit(_where)/select_n | solution.py:34
  331.2 6.3 %fusion.73 = f32[64,128,128]{2,1,0:T(8,128)} fusion(f32[64,128,128]{2,1,0:T(8,128)} %get-tuple-element.576, bf16[4,64,128,128]{3,2,1,0:T(8,128)(2,1)} %get-tuple-element.588, s32[]{:T(128)S(6)} %select_n.103, f32[64]{0:T(128)S(1)} %bitcast_convert_fusion.4, pred[]{:T(512)S(6)} %compare.7, pred[]{:T(512)S(6)} %gt.12), kind=kLoop, calls=%fused_computation.1.clone.1 | loop fusion | flops 5242880 | bytes 10486022 | tf_op jit(solution)/shard_map/while/body/eval_jaxpr/jit(_where)/select_n | solution.py:34
  337.5 6.1 %fusion.73 = f32[64,128,128]{2,1,0:T(8,128)} fusion(f32[64,128,128]{2,1,0:T(8,128)} %get-tuple-element.576, bf16[4,64,128,128]{3,2,1,0:T(8,128)(2,1)} %get-tuple-element.588, s32[]{:T(128)S(6)} %select_n.103, f32[64]{0:T(128)S(1)} %bitcast_convert_fusion.4, pred[]{:T(512)S(6)} %compare.7, pred[]{:T(512)S(6)} %gt.12), kind=kLoop, calls=%fused_computation.1.clone.1 | loop fusion | flops 5242880 | bytes 10486022 | tf_op jit(solution)/shard_map/while/body/eval_jaxpr/jit(_where)/select_n | solution.py:34
  343.6 6.0 %fusion.73 = f32[64,128,128]{2,1,0:T(8,128)} fusion(f32[64,128,128]{2,1,0:T(8,128)} %get-tuple-element.576, bf16[4,64,128,128]{3,2,1,0:T(8,128)(2,1)} %get-tuple-element.588, s32[]{:T(128)S(6)} %select_n.103, f32[64]{0:T(128)S(1)} %bitcast_convert_fusion.4, pred[]{:T(512)S(6)} %compare.7, pred[]{:T(512)S(6)} %gt.12), kind=kLoop, calls=%fused_computation.1.clone.1 | loop fusion | flops 5242880 | bytes 10486022 | tf_op jit(solution)/shard_map/while/body/eval_jaxpr/jit(_where)/select_n | solution.py:34
  349.6 2.7 convert_element_type.255
  352.3 0.7 copy-done.4
  353.2 6.1 %fusion.12 = (f32[256,4,16]{0,2,1:T(8,128)}, bf16[256,4,128]{0,2,1:T(8,128)(2,1)}) fusion(f32[256,4,128]{0,2,1:T(8,128)S(1)} %copy-done.8, f32[256,4,16]{0,2,1:T(8,128)S(1)} %bitcast.161, bf16[4,16,128,128]{3,2,1,0:T(8,128)(2,1)S(1)} %bitcast.136, bf16[256,4,16,128]{3,2,1,0:T(8,128)(2,1)S(1)} %bitcast.148), kind=kOutput, calls=%fused_computation.25 | convolution fusion | flops 549306368 | bytes 7208960 | tf_op jit(solution)/shard_map/transpose(jvp())/while/body/eval_jaxpr/sgkp,sgkn->gkpn/dot_general | solution.py:59
  359.2 0.9 copy.169
  360.2 2.4 multiply_reduce_fusion.1
  362.8 2.5 reduce-window.24
  365.3 1.2 fusion.49
  366.5 8.6 %fusion.21 = bf16[256,4,16,128]{0,3,2,1:T(8,128)(2,1)} fusion(bf16[256,4,16,128]{0,3,2,1:T(8,128)(2,1)} %bitcast.144, bf16[4,16,256,128]{2,3,1,0:T(8,128)(2,1)} %fusion.8, f32[4,16]{1,0:T(4,128)S(1)} %mul.237, bf16[4,16,128,128]{3,2,1,0:T(8,128)(2,1)} %bitcast.137, f32[256,4,16]{0,2,1:T(8,128)} %bitcast.160, f32[256,4,128]{0,2,1:T(8,128)} %copy-done.7), kind=kOutput, calls=%fused_computation.39 | convolution fusion | flops 553648128 | bytes 15270144 | tf_op jit(solution)/shard_map/transpose(jvp())/while/body/eval_jaxpr/sgkp,sgkn->gkpn/dot_general | solution.py:59
  375.3 6.3 %copy.175 = bf16[1,256,8192]{2,1,0:T(8,128)(2,1)} copy(bf16[1,256,8192]{1,2,0:T(8,128)(2,1)} %bitcast.149) | data formatting | bytes 8388608
  381.6 0.8 copy.176
  382.6 0.7 reduce_window_sum.61
  383.3 50.2 %all-reduce.4.cloned.1.call-done = bf16[512,512]{0,1:T(8,128)(2,1)} async-done(((bf16[512,512]{0,1:T(8,128)(2,1)}), bf16[512,512]{0,1:T(8,128)(2,1)}) %all-reduce.4.cloned.1.call-update) | async-done | bytes 524304 | tf_op jit(solution)/shard_map/psum | solution.py:166
  433.5 1.2 convert_multiply_fusion.2
  434.7 1.3 copy.177
  (91 shorter events, 4.9 us)
Async XLA Ops:
  7.2 207.9 %all-gather.6.cloned.1.call-start = ((), (), s32[]{:S(2)}) async-start(), calls=%async_computation.3 | async-start | bytes 10485760 | tf_op jit(solution)/shard_map/all_gather | solution.py:18
  10.4 3.7 copy-start.11
  10.4 3.6 copy-start.7
  14.0 4.9 %copy-start.3 = (bf16[32,8,64,128]{3,2,1,0:T(8,128)(2,1)}, bf16[32,8,64,128]{3,2,1,0:T(8,128)(2,1)S(1)}, u32[]{:S(2)}) copy-start(bf16[32,8,64,128]{3,2,1,0:T(8,128)(2,1)S(1)} %copy.186) | copy-start | bytes 12582916
  18.9 3.0 copy-start.6
  25.9 132.2 %all-to-all-start = ((bf16[16,512,512]{2,1,0:T(8,128)(2,1)}), bf16[16,512,512]{2,1,0:T(8,128)(2,1)}, u32[]{:S(2)}, u32[]{:S(2)}) async-start(bf16[16,512,512]{2,1,0:T(8,128)(2,1)} %stack.2), calls=%async_computation | async-start | bytes 16777216 | tf_op jit(solution)/shard_map/all_to_all | solution.py:131
  34.1 292.4 %all-gather.4.cloned.1.call-start = ((), (), s32[]{:S(2)}) async-start(), calls=%async_computation.2 | async-start | bytes 10485760 | tf_op jit(solution)/shard_map/all_gather | solution.py:18
  165.4 5.0 %copy-start.9 = (f32[256,4,128]{0,2,1:T(8,128)}, f32[256,4,128]{0,2,1:T(8,128)S(1)}, u32[]{:S(2)}) copy-start(f32[256,4,128]{0,2,1:T(8,128)S(1)} %copy.148) | copy-start | bytes 1572868
  170.4 4.3 copy-start.16
  174.5 200.7 %reduce-scatter.2.cloned.1.call-start = ((), (), s32[]{:S(2)}) async-start(), calls=%async_computation.4 | async-start | bytes 8912896 | tf_op jit(solution)/shard_map/reduce_scatter | solution.py:158
  197.6 1.0 copy-start.5
  237.6 3.5 copy-start.2
  237.6 3.6 copy-start.10
  241.2 3.0 copy-start.1
  249.8 0.7 copy-start.15
  249.8 183.7 %all-reduce.4.cloned.1.call-start = ((), (), s32[]{:S(2)}) async-start(), calls=%async_computation.5 | async-start | bytes 1048576 | tf_op jit(solution)/shard_map/psum | solution.py:166
  250.6 68.4 %copy-start.14 = (f32[4,16,256]{2,1,0:T(8,128)S(1)}, f32[4,16,256]{2,1,0:T(8,128)}, u32[]{:S(2)}) copy-start(f32[4,16,256]{2,1,0:T(8,128)} %get-tuple-element.473) | copy-start | bytes 196612
  319.1 7.3 %copy-start.13 = (f32[256,4,16]{0,2,1:T(8,128)S(1)}, f32[256,4,16]{0,2,1:T(8,128)}, u32[]{:S(2)}) copy-start(f32[256,4,16]{0,2,1:T(8,128)} %get-tuple-element.476) | copy-start | bytes 196612
  349.6 3.4 copy-start.4
  349.6 3.6 copy-start.8
  349.6 3.6 copy-start.12
  352.3 6.9 %copy-start = (bf16[64,128,128]{2,1,0:T(8,128)(2,1)}, bf16[64,128,128]{2,1,0:T(8,128)(2,1)S(1)}, u32[]{:S(2)}) copy-start(bf16[64,128,128]{2,1,0:T(8,128)(2,1)S(1)} %convert_element_type.255) | copy-start | bytes 6291460
Sparse Core Ops, SparseCore 0:
  22.0 85.5 all-gather.5
  174.6 83.2 all-gather.3
  261.3 86.4 reduce-scatter.1
  375.3 58.1 all-reduce.3
